TPU v7x, 256 devices: a whole 4x4x8 slice. The times are simulated.
256 devices in a mesh: pert: 2 (over x_lo), band: 16 (over z, core), pw: 8 (over x_hi, y).
Axes of the slice: x: 4 (x_hi: 2, x_lo: 2; x = x_hi * 2 + x_lo), y: 4, z: 8, core: 2. Of those that a mesh axis runs over, the one named last changes fastest.
Arguments:
- trial_potential: float32 [2, 128, 64, 128], P(None, 'pw'), may hold values from -6 to 6
- local_potential: float32 [128, 64, 128], P('pw'), may hold values from -0.5 to 0.5
- psi_coef: float32 [131072, 16], P('pw', 'band'), may hold values from -6 to 6
- band_energy: float32 [16], replicated, may hold values from -1 to -0.4
- band_slot: int32 [16], P('band'), may hold values from 0 to 15, each once
- pw_index: int32 [131072], P('pw'), may hold values from 0 to 131071, as said below
Outputs:
- density_response: float32 [2, 128, 64, 128], P('pert', 'pw', 'band')
- intersections: float32 [2, 2], replicated
Inputs may be any that keep to these rules, and one draw needn't show every extreme that they name: `pw_index`: entry j of each aligned run of 16384 entries is a cell q * 128 + kz of the line q = (j mod 16384) // 16, with kz below 128; the kz of the 16 entries of one line are distinct. `band_slot`: each band appears in exactly one slot.
All inputs are finite; a program needn't handle non-finite values.
Results may differ from a plain program's by a relative error of at most 0.0001.
Values sent between devices are 32-bit elements; how exact they have to be, the bound alone decides.
No kernel may reach another device: no remote copies, remote signals or barrier semaphores. Data moves between devices by JAX's collectives and lax.ppermute only.
A program may use at most 192 MiB of HBM per device.

v0:
```python
import math

import jax
import jax.numpy as jnp
from jax import lax
from jax.sharding import PartitionSpec as P

NP_DEV = 1
ITERS = 3


highest = lax.Precision.HIGHEST


def hartley_table(points):
    wave_index = jnp.arange(points, dtype=jnp.int32)
    phase_table = wave_index[:, None] * wave_index[None, :] % points
    angles = phase_table.astype(jnp.float32) * (2.0 * math.pi / points)
    return (jnp.cos(angles) + jnp.sin(angles)) / math.sqrt(points)


def wave_energy(wave_number, points):
    folded = jnp.minimum(wave_number, points - wave_number).astype(jnp.float32)
    return 4.0 * (folded / points) ** 2


def line_table(index_values, line_count, per_line, size_z):
    depth = (index_values % size_z).reshape(line_count, per_line)
    cells = jnp.arange(size_z, dtype=jnp.int32)
    return (depth[:, :, None] == cells[None, None, :]).astype(jnp.float32)


def place_block(coefficients, table, size_x, slab_y, size_z):
    batch_count = coefficients.shape[0]
    line_count, per_line, depth = table.shape
    lined = coefficients.reshape(batch_count, line_count, per_line)
    block = jnp.einsum("flc,lcz->flz", lined, table, precision=highest)
    return block.reshape(batch_count, size_x, slab_y, size_z)


def read_block(block, table):
    batch_count = block.shape[0]
    line_count, per_line, depth = table.shape
    lined = block.reshape(batch_count, line_count, depth)
    values = jnp.einsum("flz,lcz->flc", lined, table, precision=highest)
    return values.reshape(batch_count, line_count * per_line)


def per_device(trial_potential, local_potential, psi_coef, band_energy, band_slot, pw_index):
    pw_count = lax.axis_size("pw")
    band_count = lax.axis_size("band")
    slab_x, size_y, size_z = local_potential.shape
    size_x = slab_x * pw_count
    slab_y = size_y // pw_count
    bands_here = psi_coef.shape[1]
    coef_count = psi_coef.shape[0]
    coef_total = coef_count * pw_count
    total_bands = band_energy.shape[0]
    total_perts = trial_potential.shape[0]
    functions = NP_DEV * bands_here
    line_count = size_x * slab_y
    per_line = coef_count // line_count
    table_x = hartley_table(size_x)
    table_y = hartley_table(size_y)
    table_z = hartley_table(size_z)
    own_trials = lax.dynamic_slice_in_dim(
        trial_potential, lax.axis_index("pert") * NP_DEV, NP_DEV, 0
    )
    wave_x = pw_index // (slab_y * size_z)
    wave_y = lax.axis_index("pw") * slab_y + pw_index // size_z % slab_y
    wave_z = pw_index % size_z
    kinetic = (
        wave_energy(wave_x, size_x) + wave_energy(wave_y, size_y) + wave_energy(wave_z, size_z)
    )
    matches = band_slot[:, None] == jnp.arange(total_bands, dtype=jnp.int32)[None, :]
    energies = jnp.sum(jnp.where(matches, band_energy[None, :], 0.0), axis=1)

    def apply_x(members):
        return jnp.einsum("fxyz,xa->fayz", members, table_x, precision=highest)

    def apply_yz(members):
        members = jnp.einsum("fxyz,ya->fxaz", members, table_y, precision=highest)
        return jnp.einsum("fxyz,za->fxya", members, table_z, precision=highest)

    own_table = line_table(pw_index, line_count, per_line, size_z)

    def to_grid(coefficients):
        coef_block = place_block(coefficients, own_table, size_x, slab_y, size_z)
        coef_block = apply_x(coef_block)
        return apply_yz(lax.all_to_all(coef_block, "pw", split_axis=1, concat_axis=2, tiled=True))

    def to_coeffs(fields):
        coef_block = apply_x(
            lax.all_to_all(apply_yz(fields), "pw", split_axis=2, concat_axis=1, tiled=True)
        )
        return read_block(coef_block, own_table)

    psi_all = lax.all_gather(psi_coef, "band", axis=1, tiled=True)

    def project(values):
        intersection = jnp.dot(values, psi_all, precision=highest)
        intersection = lax.psum(intersection, "pw")
        return values - jnp.dot(intersection, psi_all.T, precision=highest) / coef_total

    psi_grid = to_grid(psi_coef.T)
    products = (own_trials[:, None] * psi_grid[None]).reshape((functions,) + psi_grid.shape[1:])
    driving = -project(to_coeffs(products))
    band_levels = jnp.tile(energies, NP_DEV)[:, None]
    inverse_diag = 1.0 / (kinetic[None, :] - band_levels)
    response = inverse_diag * driving
    for iteration in range(ITERS):
        potential_part = to_coeffs(local_potential[None] * to_grid(response))
        applied = kinetic[None, :] * response + potential_part - band_levels * response
        response = response + inverse_diag * (driving - project(applied))
    response_grid = to_grid(response).reshape((NP_DEV, bands_here) + psi_grid.shape[1:])
    density_part = 2.0 * jnp.sum(psi_grid[None] * response_grid, axis=1)
    rows_band = size_y // band_count
    summed = lax.psum(density_part, "band")
    density_rows = lax.dynamic_slice_in_dim(
        summed, lax.axis_index("band") * rows_band, rows_band, 2
    )
    band_rows = lax.dynamic_slice_in_dim(
        trial_potential, lax.axis_index("band") * rows_band, rows_band, 2
    )
    partial_cols = jnp.einsum("ixyz,jxyz->ij", band_rows, density_rows, precision=highest)
    placed = lax.dynamic_update_slice_in_dim(
        jnp.zeros((total_perts, total_perts), jnp.float32),
        partial_cols,
        lax.axis_index("pert") * NP_DEV,
        1,
    )
    intersections = lax.psum(placed, ("pert", "band", "pw")) / (total_bands * coef_total)
    return (density_rows, intersections)


def solution(mesh):
    return jax.shard_map(
        per_device,
        mesh=mesh,
        in_specs=(
            P(None, "pw", None, None),
            P("pw", None, None),
            P("pw", "band"),
            P(),
            P("band"),
            P("pw"),
        ),
        out_specs=(P("pert", "pw", "band", None), P()),
        check_vma=False,
    )
```

profile of v0, /device:TPU:2, one launch (start us, length us, event | category | flops | bytes accessed | tf_op | source)
XLA Modules:
  0.0 537.1 jit_solution(15503619558301353716)
XLA Ops:
  10.6 7.4 %fusion.8 = f32[1024,1,128]{2,1,0:T(1,128)S(1)} fusion(f32[1024,16,1]{1,2,0:T(1,128)S(1)} %bitcast.350, s32[1024,16]{1,0:T(8,128)S(1)} %eq.35), kind=kOutput, calls=%fused_computation.9 | convolution fusion | flops 27262976 | bytes 655360 | tf_op jit(solution)/shard_map/flc,lcz->flz/dot_general | solution.py:37
  26.8 10.3 %all-to-all-done = f32[1,128,8,128]{3,2,0,1:T(8,128)S(1)} async-done(((f32[1,128,8,128]{3,2,0,1:T(8,128)}), f32[1,128,8,128]{3,2,0,1:T(8,128)S(1)}, u32[]{:S(2)}, u32[]{:S(2)}) %all-to-all-start) | async-done | bytes 524320 | tf_op jit(solution)/shard_map/all_to_all | solution.py:90
  46.3 9.7 %all-to-all-done.1 = f32[1,16,64,128]{3,1,0,2:T(8,128)S(1)} async-done(((f32[1,16,64,128]{3,1,0,2:T(8,128)}), f32[1,16,64,128]{3,1,0,2:T(8,128)S(1)}, u32[]{:S(2)}, u32[]{:S(2)}) %all-to-all-start.1) | async-done | bytes 524320 | tf_op jit(solution)/shard_map/all_to_all | solution.py:94
  57.2 9.3 %fusion.7 = f32[1024,1,16]{2,1,0:T(1,128)S(1)} fusion(f32[1024,128,1]{1,2,0:T(1,128)S(1)} %bitcast.359, s32[1024,16]{1,0:T(8,128)S(1)} %eq.35), kind=kOutput, calls=%fused_computation.8 | convolution fusion | flops 27262976 | bytes 655360 | tf_op jit(solution)/shard_map/flz,lcz->flc/dot_general | solution.py:45
  74.5 23.2 %psum.42 = f32[16]{0:T(128)S(1)} all-reduce(f32[16]{0:T(128)S(1)} %convolution_bitcast_fusion.22), channel_id=1, replica_groups=mesh['pert'=2,'band'=16,'pw'=8] {'pw'}, use_global_device_ids=true, to_apply=%region_1.2 | all-reduce | flops 16 | bytes 128 | tf_op jit(solution)/shard_map/psum | solution.py:102
  99.9 7.4 %fusion.6 = f32[1024,1,128]{2,1,0:T(1,128)S(1)} fusion(f32[1024,16,1]{1,2,0:T(1,128)S(1)} %bitcast.351, s32[1024,16]{1,0:T(8,128)S(1)} %eq.35), kind=kOutput, calls=%fused_computation.7 | convolution fusion | flops 27262976 | bytes 655360 | tf_op jit(solution)/shard_map/flc,lcz->flz/dot_general | solution.py:37
  108.6 12.9 %all_to_all.135 = f32[1,128,8,128]{3,2,0,1:T(8,128)S(1)} all-to-all(f32[1,128,8,128]{3,2,0,1:T(8,128)S(1)} %copy.65), channel_id=1, replica_groups=mesh['pert'=2,'band'=16,'pw'=8] {'pw'}, dimensions={1} | all-to-all | bytes 1048576 | tf_op jit(solution)/shard_map/all_to_all | solution.py:90
  125.0 12.7 %all_to_all.136 = f32[1,16,64,128]{3,1,0,2:T(8,128)S(1)} all-to-all(f32[1,16,64,128]{3,1,0,2:T(8,128)S(1)} %copy.67), channel_id=1, replica_groups=mesh['pert'=2,'band'=16,'pw'=8] {'pw'}, dimensions={2} | all-to-all | bytes 1048576 | tf_op jit(solution)/shard_map/all_to_all | solution.py:94
  139.0 9.3 %fusion.5 = f32[1024,1,16]{2,1,0:T(1,128)S(1)} fusion(f32[1024,128,1]{1,2,0:T(1,128)S(1)} %bitcast.361, s32[1024,16]{1,0:T(8,128)S(1)} %eq.35), kind=kOutput, calls=%fused_computation.6 | convolution fusion | flops 27262976 | bytes 655360 | tf_op jit(solution)/shard_map/flz,lcz->flc/dot_general | solution.py:45
  150.8 20.7 %psum.43 = f32[16]{0:T(128)S(1)} all-reduce(f32[16]{0:T(128)S(1)} %convolution_bitcast_fusion.21), channel_id=1, replica_groups=mesh['pert'=2,'band'=16,'pw'=8] {'pw'}, use_global_device_ids=true, to_apply=%region_2.3 | all-reduce | flops 16 | bytes 128 | tf_op jit(solution)/shard_map/psum | solution.py:102
  173.5 7.4 %fusion.4 = f32[1024,1,128]{2,1,0:T(1,128)S(1)} fusion(f32[1024,16,1]{1,2,0:T(1,128)S(1)} %bitcast.355, s32[1024,16]{1,0:T(8,128)S(1)} %eq.35), kind=kOutput, calls=%fused_computation.5 | convolution fusion | flops 27262976 | bytes 655360 | tf_op jit(solution)/shard_map/flc,lcz->flz/dot_general | solution.py:37
  182.2 13.7 %all_to_all.137 = f32[1,128,8,128]{3,2,0,1:T(8,128)S(1)} all-to-all(f32[1,128,8,128]{3,2,0,1:T(8,128)S(1)} %copy.73), channel_id=1, replica_groups=mesh['pert'=2,'band'=16,'pw'=8] {'pw'}, dimensions={1} | all-to-all | bytes 1048576 | tf_op jit(solution)/shard_map/all_to_all | solution.py:90
  199.3 12.5 %all_to_all.138 = f32[1,16,64,128]{3,1,0,2:T(8,128)S(1)} all-to-all(f32[1,16,64,128]{3,1,0,2:T(8,128)S(1)} %copy.75), channel_id=1, replica_groups=mesh['pert'=2,'band'=16,'pw'=8] {'pw'}, dimensions={2} | all-to-all | bytes 1048576 | tf_op jit(solution)/shard_map/all_to_all | solution.py:94
  213.1 9.3 %fusion.3 = f32[1024,1,16]{2,1,0:T(1,128)S(1)} fusion(f32[1024,128,1]{1,2,0:T(1,128)S(1)} %bitcast.363, s32[1024,16]{1,0:T(8,128)S(1)} %eq.35), kind=kOutput, calls=%fused_computation.4 | convolution fusion | flops 27262976 | bytes 655360 | tf_op jit(solution)/shard_map/flz,lcz->flc/dot_general | solution.py:45
  224.9 20.9 %psum.44 = f32[16]{0:T(128)S(1)} all-reduce(f32[16]{0:T(128)S(1)} %convolution_bitcast_fusion.20), channel_id=1, replica_groups=mesh['pert'=2,'band'=16,'pw'=8] {'pw'}, use_global_device_ids=true, to_apply=%region_3.4 | all-reduce | flops 16 | bytes 128 | tf_op jit(solution)/shard_map/psum | solution.py:102
  247.8 7.4 %fusion.2 = f32[1024,1,128]{2,1,0:T(1,128)S(1)} fusion(f32[1024,16,1]{1,2,0:T(1,128)S(1)} %bitcast.356, s32[1024,16]{1,0:T(8,128)S(1)} %eq.35), kind=kOutput, calls=%fused_computation.3 | convolution fusion | flops 27262976 | bytes 655360 | tf_op jit(solution)/shard_map/flc,lcz->flz/dot_general | solution.py:37
  256.4 13.8 %all_to_all.139 = f32[1,128,8,128]{3,2,0,1:T(8,128)S(1)} all-to-all(f32[1,128,8,128]{3,2,0,1:T(8,128)S(1)} %copy.81), channel_id=1, replica_groups=mesh['pert'=2,'band'=16,'pw'=8] {'pw'}, dimensions={1} | all-to-all | bytes 1048576 | tf_op jit(solution)/shard_map/all_to_all | solution.py:90
  273.8 12.7 %all_to_all.140 = f32[1,16,64,128]{3,1,0,2:T(8,128)S(1)} all-to-all(f32[1,16,64,128]{3,1,0,2:T(8,128)S(1)} %copy.83), channel_id=1, replica_groups=mesh['pert'=2,'band'=16,'pw'=8] {'pw'}, dimensions={2} | all-to-all | bytes 1048576 | tf_op jit(solution)/shard_map/all_to_all | solution.py:94
  287.7 9.3 %fusion.1 = f32[1024,1,16]{2,1,0:T(1,128)S(1)} fusion(f32[1024,128,1]{1,2,0:T(1,128)S(1)} %bitcast.365, s32[1024,16]{1,0:T(8,128)S(1)} %eq.35), kind=kOutput, calls=%fused_computation.2 | convolution fusion | flops 27262976 | bytes 655360 | tf_op jit(solution)/shard_map/flz,lcz->flc/dot_general | solution.py:45
  299.5 21.1 %psum.45 = f32[16]{0:T(128)S(1)} all-reduce(f32[16]{0:T(128)S(1)} %convolution_bitcast_fusion.19), channel_id=1, replica_groups=mesh['pert'=2,'band'=16,'pw'=8] {'pw'}, use_global_device_ids=true, to_apply=%region_4.5 | all-reduce | flops 16 | bytes 128 | tf_op jit(solution)/shard_map/psum | solution.py:102
  322.6 7.4 %fusion = f32[1024,1,128]{2,1,0:T(1,128)S(1)} fusion(f32[1024,16,1]{1,2,0:T(1,128)S(1)} %bitcast.349, s32[1024,16]{1,0:T(8,128)S(1)} %eq.35), kind=kOutput, calls=%fused_computation.1 | convolution fusion | flops 27262976 | bytes 655360 | tf_op jit(solution)/shard_map/flc,lcz->flz/dot_general | solution.py:37
  331.2 13.1 %all_to_all.141 = f32[1,128,8,128]{3,2,0,1:T(8,128)S(1)} all-to-all(f32[1,128,8,128]{3,2,0,1:T(8,128)S(1)} %copy.89), channel_id=1, replica_groups=mesh['pert'=2,'band'=16,'pw'=8] {'pw'}, dimensions={1} | all-to-all | bytes 1048576 | tf_op jit(solution)/shard_map/all_to_all | solution.py:90
  347.7 104.2 %all-reduce.2.cloned.1.call-done = f32[1,16,64,128]{3,2,1,0:T(8,128)} async-done(((f32[1,16,64,128]{3,2,1,0:T(8,128)}), f32[1,16,64,128]{3,2,1,0:T(8,128)}) %all-reduce.2.cloned.1.call-update) | async-done | bytes 524304 | tf_op jit(solution)/shard_map/psum | solution.py:118
  453.5 75.9 %psum.47 = f32[2,2]{1,0:T(2,128)S(1)} all-reduce(f32[2,2]{1,0:T(2,128)S(1)} %dynamic_update_slice.3), channel_id=1, replica_groups=mesh['pert'=2,'band'=16,'pw'=8] {'pert','band','pw'}, use_global_device_ids=true, to_apply=%region_6.7 | all-reduce | flops 4 | bytes 32 | tf_op jit(solution)/shard_map/psum | solution.py:132
  (99 shorter events, 70.0 us)
Async XLA Ops:
  20.0 17.1 %all-to-all-start = ((f32[1,128,8,128]{3,2,0,1:T(8,128)}), f32[1,128,8,128]{3,2,0,1:T(8,128)S(1)}, u32[]{:S(2)}, u32[]{:S(2)}) async-start(f32[1,128,8,128]{3,2,0,1:T(8,128)} %copy.57), calls=%async_computation | async-start | bytes 1048576 | tf_op jit(solution)/shard_map/all_to_all | solution.py:90
  26.1 45.5 %all-gather.3.cloned.1.call-start = ((), (), s32[]{:S(2)}) async-start(), calls=%async_computation.10 | async-start | bytes 1114112 | tf_op jit(solution)/shard_map/all_gather | solution.py:98
  37.1 1.6 copy-start.2
  40.3 5.3 copy-start.5
  41.5 14.5 %all-to-all-start.1 = ((f32[1,16,64,128]{3,1,0,2:T(8,128)}), f32[1,16,64,128]{3,1,0,2:T(8,128)S(1)}, u32[]{:S(2)}, u32[]{:S(2)}) async-start(f32[1,16,64,128]{3,1,0,2:T(8,128)} %copy.59), calls=%async_computation.1 | async-start | bytes 1048576 | tf_op jit(solution)/shard_map/all_to_all | solution.py:94
  45.0 406.9 %all-reduce.2.cloned.1.call-start = ((), (), s32[]{:S(2)}) async-start(), calls=%async_computation.9 | async-start | bytes 1048576 | tf_op jit(solution)/shard_map/psum | solution.py:118
  66.9 32.0 %copy-start.3 = (s32[16384]{0:T(1024)S(1)}, s32[16384]{0:T(1024)}, u32[]{:S(2)}) copy-start(s32[16384]{0:T(1024)} %param.11) | copy-start | bytes 196612
  71.5 26.2 %copy-start = (f32[16,1,16384]{2,1,0:T(1,128)S(1)}, f32[16,1,16384]{2,1,0:T(1,128)}, u32[]{:S(2)}) copy-start(f32[16,1,16384]{2,1,0:T(1,128)} %all-gather.3.cloned.1.call-done) | copy-start | bytes 3145732
  108.5 13.7 %copy-start.1 = (f32[16,64,128]{2,1,0:T(8,128)S(1)}, f32[16,64,128]{2,1,0:T(8,128)}, u32[]{:S(2)}) copy-start(f32[16,64,128]{2,1,0:T(8,128)} %param.7) | copy-start | bytes 1572868
  452.7 77.3 %copy-start.4 = (f32[1,16,4,128]{3,2,1,0:T(4,128)}, f32[1,16,4,128]{3,2,1,0:T(4,128)S(1)}, u32[]{:S(2)}) copy-start(f32[1,16,4,128]{3,2,1,0:T(4,128)S(1)} %constant_dynamic-slice_fusion.1) | copy-start | bytes 98308
Sparse Core Ops, SparseCore 0:
  28.7 42.7 all-gather.2
  346.9 104.9 all-reduce.1
where the time goes:
time: 548 us; the launch traced here: 537 us
  blocking collectives  253 us (46%)
  waiting for transfers between devices  130 us (24%)
  matrix products  110 us (20%)
  between operations  15.5 us (3%)
  local copies, waits for them, and re-layouts  10.3 us (2%)
  starting transfers between devices  9.62 us (2%)
  other arithmetic  8.53 us (2%)
    psum x1, waiting for transfers between devices, per_device(): summed = lax.psum(density_part, 'band')  104 us
    psum x4, blocking collectives, project(): intersection = lax.psum(intersection, 'pw')  85.9 us
    psum x1, blocking collectives, per_device(): lax.psum(placed, ('pert', 'band', 'pw')) / (total_bands * coef_total)  75.9 us
    all_to_all x4, blocking collectives, to_grid(): lax.all_to_all(coef_block, 'pw', split_axis=1, concat_axis=2, tiled=True)  53.5 us
    all_to_all x3, blocking collectives, to_coeffs(): lax.all_to_all(apply_yz(fields), 'pw', split_axis=2, concat_axis=1, tiled...  38 us
    dot_general x4, matrix products, read_block(): values = jnp.einsum('flz,lcz->flc', lined, table, precision=highest)  37 us
    dot_general x5, matrix products, place_block(): block = jnp.einsum('flc,lcz->flz', lined, table, precision=highest)  36.9 us
  transfers between devices with their start and end apart: 4, of which 4 were waited for; matrix products, arithmetic and copies ran while one was open for 3% of the time, Pallas kernels for 0%

commit v1 on v0

v1 whole, which is shorter than its diff:
```python
import math
from functools import partial

import jax
import jax.numpy as jnp
import numpy as np
from jax import lax
from jax.experimental import pallas as pl
from jax.experimental.pallas import tpu as pltpu
from jax.sharding import PartitionSpec as P

ITERS = 3
F32 = jnp.float32
BF16 = jnp.bfloat16
VMEM_LIMIT = 48 * 1024 * 1024


def hartley_pieces(points):
    wave_index = np.arange(points)
    angles = (wave_index[:, None] * wave_index[None, :] % points) * (2.0 * math.pi / points)
    table = (np.cos(angles) + np.sin(angles)) / math.sqrt(points)
    high = table.astype(np.float32).astype(jnp.bfloat16)
    low = (table - high.astype(np.float64)).astype(np.float32).astype(jnp.bfloat16)
    return high, low


def left_table(points):
    high, low = hartley_pieces(points)
    return np.concatenate([high, high, low], axis=1)


def right_table(points):
    high, low = hartley_pieces(points)
    return np.concatenate([high, high, low], axis=0)


def stack_pieces(values, axis):
    high = values.astype(BF16)
    low = (values - high.astype(F32)).astype(BF16)
    return jnp.concatenate([high, low, high], axis=axis)


def from_left(table, values):
    return jnp.dot(table, stack_pieces(values, 0), preferred_element_type=F32)


def from_right(values, table):
    return jnp.dot(stack_pieces(values, 1), table, preferred_element_type=F32)


def pick(values, lanes):
    return jnp.take_along_axis(values, lanes, axis=1, mode="promise_in_bounds")


def lane_numbers(shape):
    return lax.broadcasted_iota(jnp.int32, shape, len(shape) - 1)


class Sizes:
    def __init__(self, size_x, size_y, size_z, parts, per_line):
        self.x, self.y, self.z, self.parts, self.c = size_x, size_y, size_z, parts, per_line
        self.slab_x, self.slab_y = size_x // parts, size_y // parts


def send_lines(s, flat, inverse_ref, table_x, send_ref):
    for ky in range(s.slab_y):
        lanes = inverse_ref[ky]
        placed = jnp.where(lanes >= 0, pick(flat, jnp.maximum(lanes, 0)), 0.0)
        lines = from_left(table_x, placed)
        for part in range(s.parts):
            rows = lines[part * s.slab_x : (part + 1) * s.slab_x]
            send_ref[part, pl.ds(ky, s.slab_x, s.slab_y), :] = rows


def read_lines(s, recv_ref, first_row, depth, table_x):
    result = jnp.zeros((s.x, s.slab_y * s.c), F32)
    group = lane_numbers(result.shape) // s.c
    for ky in range(s.slab_y):
        lines = jnp.concatenate(
            [
                recv_ref[source, pl.ds(first_row + ky, s.slab_x, s.slab_y), :]
                for source in range(s.parts)
            ],
            axis=0,
        )
        values = pick(from_left(table_x, lines), depth)
        result = jnp.where(group == ky, values, result)
    return result


def slab_in(s, recv_ref, rows, table_y):
    lines = recv_ref[:, rows * s.slab_y : (rows + 1) * s.slab_y, :]
    return from_left(table_y, lines.reshape(s.y, s.z))


def slab_out(s, values, table_y, send_ref, first_row, rows):
    lines = from_left(table_y, values).reshape(s.parts, s.slab_y, s.z)
    start = first_row + rows * s.slab_y
    send_ref[:, start : start + s.slab_y, :] = lines


def band_dots(all_bands, flat):
    return jnp.sum(all_bands * flat[None], axis=1)


def band_sum(all_bands, weights):
    total = weights[0:1, :] * all_bands[0]
    for band in range(1, all_bands.shape[0]):
        total = total + weights[band : band + 1, :] * all_bands[band]
    return total


def total_weights(parts, coef_total):
    summed = jnp.sum(jnp.sum(parts, axis=0), axis=1, keepdims=True)
    return jnp.broadcast_to(summed * (1.0 / coef_total), parts.shape[1:])


def wave_energy(wave_number, points):
    folded = jnp.minimum(wave_number, points - wave_number).astype(F32)
    return 4.0 * (folded * (1.0 / points)) ** 2


def start_kernel(s, part_ref, slot_ref, energy_ref, psi_ref, index_ref, tx_ref,
                 send_ref, inverse_ref, depth_ref, diag_ref):
    depth = index_ref[...] % s.z
    depth_ref[...] = depth
    lanes = lane_numbers((s.x, s.z))
    for ky in range(s.slab_y):
        inverse = jnp.full((s.x, s.z), -1, jnp.int32)
        for c in range(s.c):
            lane = ky * s.c + c
            same = pick(depth, jnp.full((s.x, s.z), lane, jnp.int32))
            inverse = jnp.where(same == lanes, lane, inverse)
        inverse_ref[ky] = inverse
    wave_x = lax.broadcasted_iota(jnp.int32, depth.shape, 0)
    wave_y = part_ref[0] * s.slab_y + lane_numbers(depth.shape) // s.c
    kinetic = wave_energy(wave_x, s.x) + wave_energy(wave_y, s.y) + wave_energy(depth, s.z)
    diag_ref[...] = 1.0 / (kinetic - energy_ref[slot_ref[0]])
    send_lines(s, psi_ref[...], inverse_ref, tx_ref[...], send_ref)


def driving_kernel(s, recv_ref, trial_ref, local_ref, tyl_ref, tzr_ref,
                   send_ref, grid_ref):
    table_y, table_z = tyl_ref[...], tzr_ref[...]
    block = s.slab_x * s.slab_y
    group = 4
    for first in range(0, s.slab_x, group):
        inner = jnp.concatenate(
            [slab_in(s, recv_ref, row, table_y) for row in range(first, first + group)], axis=0
        )
        rows = pl.ds(first * s.y, group * s.y)
        grid = from_right(inner, table_z)
        grid_ref[rows, :] = grid
        for number, potential in enumerate((trial_ref[0, rows, :], local_ref[rows, :])):
            outer = from_right(potential * grid, table_z)
            for row in range(group):
                slab_out(s, outer[row * s.y : (row + 1) * s.y], table_y, send_ref,
                         number * block, first + row)


def project_kernel(s, recv_ref, depth_ref, all_ref, tx_ref, driving_ref, local_ref, dots_ref):
    depth, table_x = depth_ref[...], tx_ref[...]
    driving = read_lines(s, recv_ref, 0, depth, table_x)
    driving_ref[...] = driving
    local_ref[...] = read_lines(s, recv_ref, s.slab_x * s.slab_y, depth, table_x)
    dots = band_dots(all_ref[...], driving)
    dots_ref[...] = jnp.broadcast_to(dots[None], dots_ref.shape)


def first_kernel(s, coef_total, dots_ref, driving_ref, all_ref, diag_ref, inverse_ref, tx_ref,
                 send_ref, start_ref):
    weights = total_weights(dots_ref[...], coef_total)
    start = band_sum(all_ref[...], weights) - driving_ref[...]
    start_ref[...] = start
    send_lines(s, start * diag_ref[...], inverse_ref, tx_ref[...], send_ref)


def potential_kernel(s, dots_ref, recv_ref, local_ref, tyl_ref, tzr_ref, send_ref):
    table_y, table_z = tyl_ref[...], tzr_ref[...]
    block = s.slab_x * s.slab_y
    group = 4
    for first in range(0, s.slab_x, group):
        inner = jnp.concatenate(
            [slab_in(s, recv_ref, row, table_y) for row in range(first, first + group)], axis=0
        )
        rows = pl.ds(first * s.y, group * s.y)
        grid = from_right(inner, table_z)
        outer = from_right(local_ref[rows, :] * grid, table_z)
        for row in range(group):
            slab_out(s, outer[row * s.y : (row + 1) * s.y], table_y, send_ref, 0, first + row)
    dots = dots_ref[...]
    send_ref[:, block:, :] = jnp.broadcast_to(dots[None], (s.parts,) + dots.shape)


def dots_kernel(s, all_ref, image_ref, diag_ref, start_ref, dots_ref):
    dots_ref[...] = band_dots(all_ref[...] + diag_ref[...][None] * image_ref[...], start_ref[...])


def update_kernel(s, coef_total, last, recv_ref, start_ref, depth_ref, all_ref, image_ref,
                  diag_ref, inverse_ref, tx_ref, own_ref, other_ref, send_ref, dots_ref=None):
    block = s.slab_x * s.slab_y
    table_x = tx_ref[...]
    weights = total_weights(recv_ref[:, block:, :], coef_total)
    change = read_lines(s, recv_ref, 0, depth_ref[...], table_x)
    all_bands = all_ref[...]
    state = start_ref[...] - change + band_sum(all_bands, weights)
    response = state * diag_ref[...]
    send_lines(s, response, inverse_ref, table_x, send_ref)
    if not last:
        dots_ref[...] = band_dots(all_bands + diag_ref[...][None] * image_ref[...], state)
        return
    own = jnp.sum(own_ref[...] * response, axis=0, keepdims=True)
    other = jnp.sum(other_ref[...] * response, axis=0, keepdims=True)
    sums = jnp.concatenate([own, other, jnp.zeros((6, s.z), F32)], axis=0)
    send_ref[:, block:, :] = jnp.broadcast_to(sums[None], (s.parts,) + sums.shape)


def density_kernel(s, bands, recv_ref, grid_ref, tyl_ref, tzr_ref, send_ref):
    table_y, table_z = tyl_ref[...], tzr_ref[...]
    group = 4
    keep = s.y // bands
    for first in range(0, s.slab_x, group):
        inner = jnp.concatenate(
            [slab_in(s, recv_ref, row, table_y) for row in range(first, first + group)], axis=0
        )
        rows = pl.ds(first * s.y, group * s.y)
        density = 2.0 * grid_ref[rows, :] * from_right(inner, table_z)
        for row in range(group):
            for band in range(bands):
                start = row * s.y + band * keep
                place = (first + row) * keep
                send_ref[band, place : place + keep, :] = density[start : start + keep]
    sums = jnp.sum(recv_ref[:, s.slab_x * s.slab_y :, :], axis=0)
    send_ref[:, s.slab_x * keep :, :] = jnp.broadcast_to(sums[None], (bands,) + sums.shape)


def final_kernel(s, rows, recv_ref, density_ref, sums_ref):
    total = jnp.sum(recv_ref[...], axis=0)
    density_ref[...] = total[:rows]
    lanes = jnp.sum(total[rows:], axis=1, keepdims=True)
    sums_ref[...] = jnp.broadcast_to(lanes, sums_ref.shape)


def call(kernel, out_shape, scalars=0, name=None):
    smem = pl.BlockSpec(memory_space=pltpu.SMEM)
    vmem = pl.BlockSpec(memory_space=pltpu.VMEM)

    def run(*operands):
        return pl.pallas_call(
            kernel,
            out_shape=out_shape,
            in_specs=[smem] * scalars + [vmem] * (len(operands) - scalars),
            out_specs=jax.tree.map(lambda _: vmem, out_shape),
            compiler_params=pltpu.CompilerParams(vmem_limit_bytes=VMEM_LIMIT),
            name=name,
        )(*operands)

    return run


def shape(*sizes, dtype=F32):
    return jax.ShapeDtypeStruct(sizes, dtype)


def per_device(trial_potential, local_potential, psi_coef, band_energy, band_slot, pw_index):
    parts = lax.axis_size("pw")
    band_count = lax.axis_size("band")
    slab_x, size_y, size_z = local_potential.shape
    size_x = slab_x * parts
    coef_count = psi_coef.shape[0]
    coef_total = coef_count * parts
    total_bands = band_energy.shape[0]
    total_perts = trial_potential.shape[0]
    slab_y = size_y // parts
    s = Sizes(size_x, size_y, size_z, parts, coef_count // (size_x * slab_y))
    block = slab_x * slab_y
    flat = (size_x, slab_y * s.c)
    pert = lax.axis_index("pert")
    part = lax.axis_index("pw").reshape(1).astype(jnp.int32)

    table_x = jnp.asarray(left_table(size_x))
    table_y = jnp.asarray(left_table(size_y))
    table_z = jnp.asarray(right_table(size_z))

    def exchange(values):
        return lax.all_to_all(values, "pw", split_axis=0, concat_axis=0, tiled=True)

    psi = psi_coef.reshape(flat)
    all_psi = lax.all_gather(psi, "band", axis=0)
    send, inverse, depth, diag = call(
        partial(start_kernel, s),
        (
            shape(parts, block, size_z),
            shape(slab_y, size_x, size_z, dtype=jnp.int32),
            shape(*flat, dtype=jnp.int32),
            shape(*flat),
        ),
        3,
        "start",
    )(part, band_slot, band_energy, psi, pw_index.reshape(flat), table_x)
    recv = exchange(send)

    local = local_potential.reshape(slab_x * size_y, size_z)
    trials = trial_potential.reshape(total_perts, slab_x * size_y, size_z)
    trial = lax.dynamic_slice_in_dim(trials, pert, 1, 0)
    send, psi_grid = call(
        partial(driving_kernel, s),
        (shape(parts, 2 * block, size_z), shape(slab_x * size_y, size_z)),
        0,
        "driving",
    )(recv, trial, local, table_y, table_z)
    recv = exchange(send)

    driving, image, dots = call(
        partial(project_kernel, s),
        (shape(*flat), shape(*flat), shape(parts, total_bands, size_z)),
        0,
        "project",
    )(recv, depth, all_psi, table_x)
    all_image = lax.all_gather(image, "band", axis=0)
    other = lax.ppermute(driving, "pert", [(0, 1), (1, 0)])
    dots = exchange(dots)
    send, start = call(
        partial(first_kernel, s, coef_total),
        (shape(parts, block, size_z), shape(*flat)),
        0,
        "first",
    )(dots, driving, all_psi, diag, inverse, table_x)
    for iteration in range(ITERS):
        last = iteration == ITERS - 1
        recv = exchange(send)
        if iteration == 0:
            dots = call(partial(dots_kernel, s), shape(total_bands, size_z), 0, "dots")(
                all_psi, all_image, diag, start
            )
        send = call(
            partial(potential_kernel, s),
            shape(parts, block + total_bands, size_z),
            0,
            "potential",
        )(dots, recv, local, table_y, table_z)
        recv = exchange(send)
        if last:
            outs = (shape(parts, block + 8, size_z),)
        else:
            outs = (shape(parts, block, size_z), shape(total_bands, size_z))
        send, *rest = call(partial(update_kernel, s, coef_total, last), outs, 0, "update")(
            recv, start, depth, all_psi, all_image, diag, inverse, table_x, driving, other
        )
        dots = rest[0] if rest else None

    recv = exchange(send)
    rows = slab_x * (size_y // band_count)
    send = call(
        partial(density_kernel, s, band_count),
        shape(band_count, rows + 8, size_z),
        0,
        "density",
    )(recv, psi_grid, table_y, table_z)
    recv = lax.all_to_all(send, "band", split_axis=0, concat_axis=0, tiled=True)
    density, sums = call(
        partial(final_kernel, s, rows), (shape(rows, size_z), shape(8, size_z)), 0, "final"
    )(recv)
    own = sums[:2, 0] * (2.0 / (total_bands * coef_total))
    across = lax.ppermute(own, "pert", [(0, 1), (1, 0)])
    first = jnp.stack([own, across[::-1]], axis=1)
    second = jnp.stack([across, own[::-1]], axis=1)
    intersections = jnp.where(pert == 0, first, second)
    return (
        density.reshape(1, slab_x, size_y // band_count, size_z),
        intersections,
    )


def solution(mesh):
    return jax.shard_map(
        per_device,
        mesh=mesh,
        in_specs=(
            P(None, "pw", None, None),
            P("pw", None, None),
            P("pw", "band"),
            P(),
            P("band"),
            P("pw"),
        ),
        out_specs=(P("pert", "pw", "band", None), P()),
        check_vma=False,
    )
```

time: 548 us -> 245 us (0.45); the launches traced: 537 us -> 241 us
  blocking collectives: 253 us -> 99.6 us
  matrix products: 110 us -> 0 us
  waiting for transfers between devices: 130 us -> 63.4 us
  Pallas kernels: 0 us -> 24.6 us
  starting transfers between devices: 9.62 us -> 23.3 us
  other arithmetic: 8.53 us -> 0.76 us
    psum x5 -> x0, blocking collectives: 162 us -> none  [the longest x4 85.9 us: project(): intersection = lax.psum(intersection, 'pw')]
    dot_general x45 -> x0, matrix products: 110 us -> none  [the longest x4 37 us: read_block(): values = jnp.einsum('flz,lcz->flc', lined, table, precision=highest)]
    psum x1 -> x0, waiting for transfers between devices: 104 us -> none  [per_device(): summed = lax.psum(density_part, 'band')]
    pallas_call x0 -> x13, Pallas kernels: none -> 24.6 us  [run(): pl.pallas_call(kernel, out_shape=out_shape, in_specs=[smem] * scalars + [...]
    all_gather x1 -> x2, waiting for transfers between devices: 4.59 us -> 22.2 us  [the longest x1 22.2 us: per_device(): all_image = lax.all_gather(image, 'band', axis=0)]
    unnamed x13 -> x62, local copies, waits for them, and re-layouts: 0.54 us -> 13.8 us
    ppermute x0 -> x2, waiting for transfers between devices: none -> 11 us  [the longest x1 8.75 us: per_device(): other = lax.ppermute(driving, 'pert', [(0, 1), (1, 0)])]
    all_to_all x2 -> x4, starting transfers between devices: 9.55 us -> 20.4 us  [the longest x3 16 us: exchange(): return lax.all_to_all(values, 'pw', split_axis=0, concat_axis=0, tiled=True)]
  transfers between devices with their start and end apart: 4 -> 8, of which waited for: 4 -> 6; matrix products, arithmetic and copies ran while one was open for 3% -> 0% of each run, Pallas kernels for 0% -> 3%
where the time goes in v1:
time: 245 us; the launch traced here: 241 us
  blocking collectives  99.6 us (41%)
  waiting for transfers between devices  63.4 us (26%)
  Pallas kernels  24.6 us (10%)
  starting transfers between devices  23.3 us (10%)
  between operations  15 us (6%)
  local copies, waits for them, and re-layouts  14.3 us (6%)
    all_to_all x7, blocking collectives, exchange(): return lax.all_to_all(values, 'pw', split_axis=0, concat_axis=0, tiled=True)  99.6 us
    pallas_call x13, Pallas kernels, run(): pl.pallas_call(kernel, out_shape=out_shape, in_specs=[smem] * scalars + [...  24.6 us
    all_gather x1, waiting for transfers between devices, per_device(): all_image = lax.all_gather(image, 'band', axis=0)  22.2 us
    all_to_all x1, waiting for transfers between devices, per_device(): recv = lax.all_to_all(send, 'band', split_axis=0, concat_axis=0, tiled=True)  17.2 us
    all_to_all x3, starting transfers between devices, exchange(): return lax.all_to_all(values, 'pw', split_axis=0, concat_axis=0, tiled=True)  16 us
    unnamed x62, local copies, waits for them, and re-layouts  13.8 us
    all_to_all x3, waiting for transfers between devices, exchange(): return lax.all_to_all(values, 'pw', split_axis=0, concat_axis=0, tiled=True)  12.3 us
    ppermute x1, waiting for transfers between devices, per_device(): other = lax.ppermute(driving, 'pert', [(0, 1), (1, 0)])  8.75 us
  transfers between devices with their start and end apart: 8, of which 6 were waited for; matrix products, arithmetic and copies ran while one was open for 0% of the time, Pallas kernels for 3%

profile of v1, /device:TPU:2, one launch (start us, length us, event | category | flops | bytes accessed | tf_op | source)
XLA Modules:
  0.0 240.9 jit_solution(2282661923056370923)
XLA Ops:
  11.0 4.5 %start.1 = (f32[8,128,128]{2,1,0:T(8,128)}, s32[8,128,128]{2,1,0:T(8,128)S(1)}, s32[128,128]{1,0:T(8,128)S(1)}, f32[128,128]{1,0:T(8,128)S(1)}) custom-call(s32[1]{0:T(128)} %bitcast.1.part_ref, s32[1]{0:T(128)S(6)} %copy.20.slot_ref, f32[16]{0:T(128)S(1)} %copy-done.30, f32[128,128]{1,0:T(8,128)S(1)} %bitcast.22, s32[128,128]{1,0:T(8,128)S(1)} %bitcast.23, ...), custom_call_target="tpu_custom_call" | custom-call | tf_op jit(solution)/shard_map/start/pallas_call | solution.py:249
  15.5 6.0 %all-to-all-start = ((f32[8,128,128]{2,1,0:T(8,128)}), f32[8,128,128]{2,1,0:T(8,128)S(1)}, u32[]{:S(2)}, u32[]{:S(2)}) async-start(f32[8,128,128]{2,1,0:T(8,128)} %get-tuple-element.19), calls=%async_computation | async-start | bytes 1048576 | tf_op jit(solution)/shard_map/all_to_all | solution.py:286
  21.6 10.9 %all-to-all-done.recv_ref = f32[8,128,128]{2,1,0:T(8,128)S(1)} async-done(((f32[8,128,128]{2,1,0:T(8,128)}), f32[8,128,128]{2,1,0:T(8,128)S(1)}, u32[]{:S(2)}, u32[]{:S(2)}) %all-to-all-start) | async-done | bytes 524320 | tf_op jit(solution)/shard_map/all_to_all | solution.py:286
  32.6 2.9 %driving.1 = (f32[8,256,128]{2,1,0:T(8,128)S(1)}, f32[1024,128]{1,0:T(8,128)S(1)}) custom-call(f32[8,128,128]{2,1,0:T(8,128)S(1)} %all-to-all-done.recv_ref, f32[1,1024,128]{2,1,0:T(8,128)S(1)} %constant_dynamic-slice_fusion.trial_ref, f32[1024,128]{1,0:T(8,128)S(1)} %bitcast.17, bf16[64,192]{1,0:T(8,128)(2,1)S(1)} %copy-done.19, bf16[384,128]{1,0:T(8,128)(2,1)S(1)} %copy-done.14), custom_call_target="tpu_custom_call" | custom-call | tf_op jit(solution)/shard_map/driving/pallas_call | solution.py:249
  36.3 20.7 %all_to_all.55.recv_ref = f32[8,256,128]{2,1,0:T(8,128)} all-to-all(f32[8,256,128]{2,1,0:T(8,128)S(1)} %get-tuple-element.20), channel_id=1, replica_groups=mesh['pert'=2,'band'=16,'pw'=8] {'pw'}, dimensions={0} | all-to-all | bytes 2097152 | tf_op jit(solution)/shard_map/all_to_all | solution.py:286
  59.4 1.7 project.1
  61.1 10.3 %all_to_all.56.dots_ref = f32[8,16,128]{2,1,0:T(8,128)S(1)} all-to-all(f32[8,16,128]{2,1,0:T(8,128)S(1)} %get-tuple-element.24), channel_id=1, replica_groups=mesh['pert'=2,'band'=16,'pw'=8] {'pw'}, dimensions={0} | all-to-all | bytes 131072 | tf_op jit(solution)/shard_map/all_to_all | solution.py:286
  73.1 4.2 %all-to-all-start.3 = ((f32[8,128,128]{2,1,0:T(8,128)}), f32[8,128,128]{2,1,0:T(8,128)}, u32[]{:S(2)}, u32[]{:S(2)}) async-start(f32[8,128,128]{2,1,0:T(8,128)} %copy-done.27), calls=%async_computation.3 | async-start | bytes 1048576 | tf_op jit(solution)/shard_map/all_to_all | solution.py:286
  77.3 22.2 %all-gather.6.cloned.1.call-done = f32[2048,128]{1,0:T(8,128)} async-done(((f32[128,128]{1,0:T(8,128)}), f32[2048,128]{1,0:T(8,128)}) %all-gather.6.cloned.1.call-update) | async-done | bytes 1048592 | tf_op jit(solution)/shard_map/all_gather | solution.py:320
  102.9 3.1 %potential.3 = f32[8,144,128]{2,1,0:T(8,128)S(1)} custom-call(f32[16,128]{1,0:T(8,128)S(1)} %dots.1.dots_ref, f32[8,128,128]{2,1,0:T(8,128)} %all-to-all-done.3.recv_ref, f32[1024,128]{1,0:T(8,128)S(1)} %bitcast.18, bf16[64,192]{1,0:T(8,128)(2,1)S(1)} %copy-done.20, bf16[384,128]{1,0:T(8,128)(2,1)S(1)} %copy-done.14), custom_call_target="tpu_custom_call" | custom-call | tf_op jit(solution)/shard_map/potential/pallas_call | solution.py:249
  106.8 5.8 %all-to-all-start.4 = ((f32[8,144,128]{2,1,0:T(8,128)}), f32[8,144,128]{2,1,0:T(8,128)}, u32[]{:S(2)}, u32[]{:S(2)}) async-start(f32[8,144,128]{2,1,0:T(8,128)} %copy-done.15), calls=%async_computation.4 | async-start | bytes 1179648 | tf_op jit(solution)/shard_map/all_to_all | solution.py:286
  114.0 8.8 %collective-permute-done.other_ref = f32[128,128]{1,0:T(8,128)S(1)} collective-permute-done((f32[128,128]{1,0:T(8,128)S(1)}, f32[128,128]{1,0:T(8,128)S(1)}, u32[]{:S(2)}, u32[]{:S(2)}) %collective-permute-start) | collective-permute-done | bytes 65568 | tf_op jit(solution)/shard_map/ppermute | solution.py:321
  127.5 2.4 %update.3 = (f32[8,128,128]{2,1,0:T(8,128)S(1)}, f32[16,128]{1,0:T(8,128)S(1)}) custom-call(f32[8,144,128]{2,1,0:T(8,128)} %all-to-all-done.4.recv_ref, f32[128,128]{1,0:T(8,128)S(1)} %copy-done.17, s32[128,128]{1,0:T(8,128)S(1)} %get-tuple-element.21.depth_ref, f32[16,128,128]{2,1,0:T(8,128)S(1)} %copy-done.2, f32[16,128,128]{2,1,0:T(8,128)S(1)} %bitcast.14, ...), custom_call_target="tpu_custom_call" | custom-call | tf_op jit(solution)/shard_map/update/pallas_call | solution.py:249
  130.0 15.8 %all_to_all.57.recv_ref = f32[8,128,128]{2,1,0:T(8,128)S(1)} all-to-all(f32[8,128,128]{2,1,0:T(8,128)S(1)} %get-tuple-element.30), channel_id=1, replica_groups=mesh['pert'=2,'band'=16,'pw'=8] {'pw'}, dimensions={0} | all-to-all | bytes 1048576 | tf_op jit(solution)/shard_map/all_to_all | solution.py:286
  145.8 2.0 potential.4
  147.8 13.8 %all_to_all.58.recv_ref = f32[8,144,128]{2,1,0:T(8,128)S(1)} all-to-all(f32[8,144,128]{2,1,0:T(8,128)S(1)} %potential.4), channel_id=1, replica_groups=mesh['pert'=2,'band'=16,'pw'=8] {'pw'}, dimensions={0} | all-to-all | bytes 1179648 | tf_op jit(solution)/shard_map/all_to_all | solution.py:286
  163.1 12.5 %all_to_all.59.recv_ref = f32[8,128,128]{2,1,0:T(8,128)S(1)} all-to-all(f32[8,128,128]{2,1,0:T(8,128)S(1)} %get-tuple-element.32), channel_id=1, replica_groups=mesh['pert'=2,'band'=16,'pw'=8] {'pw'}, dimensions={0} | all-to-all | bytes 1048576 | tf_op jit(solution)/shard_map/all_to_all | solution.py:286
  175.6 2.0 potential.5
  177.6 13.3 %all_to_all.60.recv_ref = f32[8,144,128]{2,1,0:T(8,128)S(1)} all-to-all(f32[8,144,128]{2,1,0:T(8,128)S(1)} %potential.5), channel_id=1, replica_groups=mesh['pert'=2,'band'=16,'pw'=8] {'pw'}, dimensions={0} | all-to-all | bytes 1179648 | tf_op jit(solution)/shard_map/all_to_all | solution.py:286
  192.1 13.1 %all_to_all.61.recv_ref = f32[8,136,128]{2,1,0:T(8,128)S(1)} all-to-all(f32[8,136,128]{2,1,0:T(8,128)S(1)} %update.5), channel_id=1, replica_groups=mesh['pert'=2,'band'=16,'pw'=8] {'pw'}, dimensions={0} | all-to-all | bytes 1114112 | tf_op jit(solution)/shard_map/all_to_all | solution.py:286
  205.2 1.7 density.1
  207.0 4.5 %all-to-all-start.10 = ((f32[16,72,128]{2,1,0:T(8,128)}), f32[16,72,128]{2,1,0:T(8,128)S(1)}, u32[]{:S(2)}, u32[]{:S(2)}) async-start(f32[16,72,128]{2,1,0:T(8,128)} %density.1), calls=%async_computation.10 | async-start | bytes 1179648 | tf_op jit(solution)/shard_map/all_to_all | solution.py:360
  211.4 17.2 %all-to-all-done.10.recv_ref = f32[16,72,128]{2,1,0:T(8,128)S(1)} async-done(((f32[16,72,128]{2,1,0:T(8,128)}), f32[16,72,128]{2,1,0:T(8,128)S(1)}, u32[]{:S(2)}, u32[]{:S(2)}) %all-to-all-start.10) | async-done | bytes 589856 | tf_op jit(solution)/shard_map/all_to_all | solution.py:360
  230.9 2.2 collective-permute-done.1
  (86 shorter events, 24.3 us)
Async XLA Ops:
  7.2 14.4 %copy-start = (f32[2,16,64,128]{3,2,1,0:T(8,128)S(1)}, f32[2,16,64,128]{3,2,1,0:T(8,128)}, u32[]{:S(2)}) copy-start(f32[2,16,64,128]{3,2,1,0:T(8,128)} %param.9) | copy-start | bytes 3145732
  7.2 1.4 copy-start.28
  7.2 49.8 %all-gather.4.cloned.1.call-start = ((), (), s32[]{:S(2)}) async-start(), calls=%async_computation.11 | async-start | bytes 1114112 | tf_op jit(solution)/shard_map/all_gather | solution.py:289
  15.4 56.1 %copy-start.8 = (s32[8,128,128]{2,1,0:T(8,128)}, s32[8,128,128]{2,1,0:T(8,128)S(1)}, u32[]{:S(2)}) copy-start(s32[8,128,128]{2,1,0:T(8,128)S(1)} %get-tuple-element.26.inverse_ref) | copy-start | bytes 1572868
  15.5 17.1 %all-to-all-start = ((f32[8,128,128]{2,1,0:T(8,128)}), f32[8,128,128]{2,1,0:T(8,128)S(1)}, u32[]{:S(2)}, u32[]{:S(2)}) async-start(f32[8,128,128]{2,1,0:T(8,128)} %get-tuple-element.19), calls=%async_computation | async-start | bytes 1048576 | tf_op jit(solution)/shard_map/all_to_all | solution.py:286
  21.5 78.0 %all-gather.6.cloned.1.call-start = ((), (), s32[]{:S(2)}) async-start(), calls=%async_computation.12 | async-start | bytes 1114112 | tf_op jit(solution)/shard_map/all_gather | solution.py:320
  21.5 11.0 %copy-start.5 = (f32[16,64,128]{2,1,0:T(8,128)S(1)}, f32[16,64,128]{2,1,0:T(8,128)}, u32[]{:S(2)}) copy-start(f32[16,64,128]{2,1,0:T(8,128)} %param.10) | copy-start | bytes 1572868
  21.6 11.0 %copy-start.14 = (bf16[384,128]{1,0:T(8,128)(2,1)S(1)}, bf16[384,128]{1,0:T(8,128)(2,1)}, u32[]{:S(2)}) copy-start(bf16[384,128]{1,0:T(8,128)(2,1)} %constant.23.clone.tzr_ref) | copy-start | bytes 294916
  21.6 11.0 %copy-start.19 = (bf16[64,192]{1,0:T(8,128)(2,1)S(1)}, bf16[64,192]{1,0:T(8,128)(2,1)}, u32[]{:S(2)}) copy-start(bf16[64,192]{1,0:T(8,128)(2,1)} %constant.22.clone.tyl_ref) | copy-start | bytes 73732
  36.3 20.7 %copy-start.13 = (bf16[128,384]{1,0:T(8,128)(2,1)S(1)}, bf16[128,384]{1,0:T(8,128)(2,1)}, u32[]{:S(2)}) copy-start(bf16[128,384]{1,0:T(8,128)(2,1)} %constant.21.clone.tx_ref) | copy-start | bytes 294916
  59.4 12.1 %copy-start.2 = (f32[16,128,128]{2,1,0:T(8,128)S(1)}, f32[16,128,128]{2,1,0:T(8,128)}, u32[]{:S(2)}) copy-start(f32[16,128,128]{2,1,0:T(8,128)} %all-gather.4.cloned.1.call-done.all_ref) | copy-start | bytes 3145732
  73.1 26.4 %copy-start.16 = (f32[128,128]{1,0:T(8,128)}, f32[128,128]{1,0:T(8,128)S(1)}, u32[]{:S(2)}) copy-start(f32[128,128]{1,0:T(8,128)S(1)} %get-tuple-element.27.start_ref) | copy-start | bytes 196612
  73.1 27.9 %all-to-all-start.3 = ((f32[8,128,128]{2,1,0:T(8,128)}), f32[8,128,128]{2,1,0:T(8,128)}, u32[]{:S(2)}, u32[]{:S(2)}) async-start(f32[8,128,128]{2,1,0:T(8,128)} %copy-done.27), calls=%async_computation.3 | async-start | bytes 1048576 | tf_op jit(solution)/shard_map/all_to_all | solution.py:286
  101.0 23.8 %copy-start.4 = (f32[2048,128]{1,0:T(8,128)S(1)}, f32[2048,128]{1,0:T(8,128)}, u32[]{:S(2)}) copy-start(f32[2048,128]{1,0:T(8,128)} %all-gather.6.cloned.1.call-done) | copy-start | bytes 3145732
  106.8 18.0 %all-to-all-start.4 = ((f32[8,144,128]{2,1,0:T(8,128)}), f32[8,144,128]{2,1,0:T(8,128)}, u32[]{:S(2)}, u32[]{:S(2)}) async-start(f32[8,144,128]{2,1,0:T(8,128)} %copy-done.15), calls=%async_computation.4 | async-start | bytes 1179648 | tf_op jit(solution)/shard_map/all_to_all | solution.py:286
  112.6 10.2 %collective-permute-start = (f32[128,128]{1,0:T(8,128)S(1)}, f32[128,128]{1,0:T(8,128)S(1)}, u32[]{:S(2)}, u32[]{:S(2)}) collective-permute-start(f32[128,128]{1,0:T(8,128)S(1)} %get-tuple-element.25.driving_ref.own_ref), channel_id=1, source_target_pairs={{0,128},{128,0},{1,129},{129,1},{2,130},{130,2},{3,131},{131,3},{4... | collective-permute-start | bytes 196616 | tf_op jit(solution)/shard_map/ppermute | solution.py:321
  130.0 15.8 %copy-start.7 = (f32[16,64,128]{2,1,0:T(8,128)S(1)}, f32[16,64,128]{2,1,0:T(8,128)}, u32[]{:S(2)}) copy-start(f32[16,64,128]{2,1,0:T(8,128)} %param.10) | copy-start | bytes 1572868
  130.0 15.8 %copy-start.21 = (bf16[64,192]{1,0:T(8,128)(2,1)S(1)}, bf16[64,192]{1,0:T(8,128)(2,1)}, u32[]{:S(2)}) copy-start(bf16[64,192]{1,0:T(8,128)(2,1)} %constant.22.clone.tyl_ref) | copy-start | bytes 73732
  147.8 13.9 %copy-start.10 = (s32[8,128,128]{2,1,0:T(8,128)S(1)}, s32[8,128,128]{2,1,0:T(8,128)}, u32[]{:S(2)}) copy-start(s32[8,128,128]{2,1,0:T(8,128)} %copy-done.8) | copy-start | bytes 1572868
  147.8 13.9 %copy-start.18 = (f32[128,128]{1,0:T(8,128)S(1)}, f32[128,128]{1,0:T(8,128)}, u32[]{:S(2)}) copy-start(f32[128,128]{1,0:T(8,128)} %copy-done.16) | copy-start | bytes 196612
  147.8 13.9 %copy-start.24 = (f32[128,128]{1,0:T(8,128)S(1)}, f32[128,128]{1,0:T(8,128)}, u32[]{:S(2)}) copy-start(f32[128,128]{1,0:T(8,128)} %copy-done.22) | copy-start | bytes 196612
  192.1 13.1 %copy-start.26 = (f32[1024,128]{1,0:T(8,128)S(1)}, f32[1024,128]{1,0:T(8,128)}, u32[]{:S(2)}) copy-start(f32[1024,128]{1,0:T(8,128)} %copy-done.25) | copy-start | bytes 1572868
  207.0 21.7 %all-to-all-start.10 = ((f32[16,72,128]{2,1,0:T(8,128)}), f32[16,72,128]{2,1,0:T(8,128)S(1)}, u32[]{:S(2)}, u32[]{:S(2)}) async-start(f32[16,72,128]{2,1,0:T(8,128)} %density.1), calls=%async_computation.10 | async-start | bytes 1179648 | tf_op jit(solution)/shard_map/all_to_all | solution.py:360
  229.6 3.5 %collective-permute-start.1 = (f32[2]{0:T(128)S(1)}, f32[2]{0:T(128)S(1)}, u32[]{:S(2)}, u32[]{:S(2)}) collective-permute-start(f32[2]{0:T(128)S(1)} %broadcast_multiply_fusion), channel_id=1, source_target_pairs={{0,128},{128,0},{1,129},{129,1},{2,130},{130,2},{3,131},{131,3},{4... | collective-permute-start | bytes 32 | tf_op jit(solution)/shard_map/ppermute | solution.py:365
  (15 other events, 13.8 us)
Sparse Core Ops, SparseCore 0:
  9.9 41.5 all-gather.3
  61.3 38.2 all-gather.5
